TPU v7x, 32 devices: a whole 2x2x4 slice. The times are simulated.
32 devices in a mesh: wa: 4 (over z), facet: 8 (over y, x, core).
Axes of the slice: x: 2, y: 2, z: 4, core: 2. Of those that a mesh axis runs over, the one named last changes fastest.
Arguments:
- visibilities: bfloat16 [4096, 2, 64], P(('wa', 'facet')), may hold values from -6 to 6
- uv_angles: float32 [4096, 2, 64], P(('wa', 'facet')), may hold values from -3.140625 to 3.140625
- routes: int32 [4096, 1], P(('wa', 'facet')), may hold values from 0 to 31; in each aligned block of 128 rows (0 to 127, 128 to 255, ...) at most 8 rows name the same one
- offsets: int32 [4096, 2], P(('wa', 'facet')), may hold values from 0 to 448
- pixel_phase: float32 [8, 512, 512], P('facet'), may hold values from -3.140625 to 3.140625
Outputs:
- partial_images: float32 [4, 8, 512, 1024], P('wa', 'facet')
Inputs may be any that keep to these rules, and one draw needn't show every extreme that they name: `routes`: the subgrids of one device name each owner at most 8 times; some owner is named exactly 8 times.
All inputs are finite; a program needn't handle non-finite values.
Results may differ from a plain program's by a relative error of at most 0.0076.
Values may be sent and summed in bfloat16 or wider, within the bound.
No kernel may reach another device: no remote copies, remote signals or barrier semaphores. Data moves between devices by JAX's collectives and lax.ppermute only.
A program may use at most 64 MiB of HBM per device.

v0:
```python
import functools
import math

import jax
import jax.numpy as jnp
import numpy as np
from jax import lax
from jax.experimental import pallas as pl
from jax.experimental.pallas import tpu as pltpu
from jax.sharding import PartitionSpec as P

SUB = 64
LANES = 128
ROWS = 8
GROUP = 8
PARTS = (7, 7, 7, 6, 5)
EARLY = 3
AHEAD = 3
LAG = 2
DIGITS = 3
DIGIT = 16.0
SINE = tuple(
    float(v)
    for v in np.linalg.lstsq(
        *(
            lambda x, w: (
                (x[:, None] ** np.arange(1, 10, 2)[None, :]) * w[:, None],
                np.sin(2 * np.pi * x) * w,
            )
        )(
            0.5 * np.cos(np.pi * (np.arange(2000) + 0.5) / 4000),
            np.ones(2000),
        ),
        rcond=None,
    )[0]
)


def sine_turns(turns):
    x = turns - jnp.round(turns)
    x2 = x * x
    total = jnp.full_like(x, SINE[-1])
    for c in SINE[-2::-1]:
        total = total * x2 + c
    return total * x


def pack_kernel(owners, cap, *refs):
    sources, out, places, sems = refs[:4], refs[4], refs[5:9], refs[9]
    copies = [
        pltpu.make_async_copy(source, place, sems.at[k])
        for k, (source, place) in enumerate(zip(sources, places))
    ]
    for copy in copies:
        copy.start()
    for copy in copies:
        copy.wait()
    routes, offsets, angles, vis = places
    rows = routes.shape[1]
    owner = lax.broadcasted_iota(jnp.int32, (owners, rows), 0)
    named = jnp.where(owner == routes[...], 1.0, 0.0)
    before = lax.broadcasted_iota(jnp.int32, (rows, rows), 0)
    until = before <= lax.broadcasted_iota(jnp.int32, (rows, rows), 1)
    until = jnp.where(until, 1.0, 0.0).astype(jnp.bfloat16)
    tally = jnp.dot(named.astype(jnp.bfloat16), until, preferred_element_type=jnp.float32)
    rank = jnp.sum(tally * named, axis=0, keepdims=True).astype(jnp.int32) - 1
    slot = routes[...] * cap + rank
    chosen = lax.broadcasted_iota(jnp.int32, (owners * cap, rows), 0) == slot
    chosen = jnp.where(chosen, 1.0, 0.0).astype(jnp.bfloat16)

    def pick(values):
        return lax.dot_general(
            chosen, values, (((1,), (1,)), ((), ())), preferred_element_type=jnp.float32
        )

    whole = angles[...]
    high = whole.astype(jnp.bfloat16)
    whole = whole - high.astype(jnp.float32)
    middle = whole.astype(jnp.bfloat16)
    low = (whole - middle.astype(jnp.float32)).astype(jnp.bfloat16)
    spot = lax.broadcasted_iota(jnp.int32, vis.shape, 0)
    digits = jnp.where(spot == 2 * DIGITS, 1, 0)
    for axis in range(2):
        for place in range(DIGITS):
            digit = (offsets[axis : axis + 1, :] >> (3 * place)) & 7
            digits = digits + jnp.where(spot == axis * DIGITS + place, digit, 0)
    digits = (digits.astype(jnp.float32) * DIGIT).astype(jnp.bfloat16)
    out[:, 0] = ((pick(high) + pick(middle)) + pick(low)).reshape(owners, cap, LANES)
    out[:, 1] = (pick(vis[...]) + pick(digits)).reshape(owners, cap, LANES)


def pack(routes, offsets, angles, vis, owners, cap):
    vmem = pl.BlockSpec(memory_space=pltpu.VMEM)
    return pl.pallas_call(
        functools.partial(pack_kernel, owners, cap),
        out_shape=pltpu.VMEM((owners, 2, cap, LANES), jnp.float32),
        compiler_params=pltpu.CompilerParams(vmem_limit_bytes=8 * 1024 * 1024),
        in_specs=[pl.BlockSpec(memory_space=pltpu.HBM)] * 4,
        out_specs=vmem,
        scratch_shapes=[
            *(pltpu.VMEM(x.shape, x.dtype) for x in (routes, offsets, angles, vis)),
            pltpu.SemaphoreType.DMA((4,)),
        ],
        name="pack",
    )(*(pltpu.with_memory_space_constraint(x, pltpu.HBM) for x in (routes, offsets, angles, vis)))


def grid_kernel(
    cells, filled, got, first_hbm, second_hbm, dense, first, second,
    turns_u, turns_v, amp_a, amp_b, grid, places, sems, *stages,
):
    slots = got.shape[0] // 2
    owners = filled.shape[0]
    cap = slots // owners
    grid_n = dense.shape[0]
    blocks = grid_n // SUB
    group = stages[0].shape[0]
    bases, lefts, rights, pieces = (stages[2 * k : 2 * k + 2] for k in range(4))
    copies = [
        pltpu.make_async_copy(first_hbm, first, sems.at[0]),
        pltpu.make_async_copy(second_hbm, second, sems.at[1]),
    ]
    for copy in copies:
        copy.start()

    lane = lax.broadcasted_iota(jnp.int32, (ROWS, LANES), 1)
    low = lane < SUB
    row = lax.broadcasted_iota(jnp.int32, (ROWS, LANES), 0)
    quarter = jnp.where(low, 0.25, 0.0).astype(jnp.float32)
    sign = jnp.where(low, -1.0, 1.0).astype(jnp.float32)
    row_f = row.astype(jnp.float32)
    upper = row < ROWS // 2
    eights = ((row & (ROWS // 2 - 1)) * ROWS + ROWS).astype(jnp.float32)
    middle = SUB // ROWS // 2

    low_cap = lax.broadcasted_iota(jnp.int32, (cap, LANES), 1) < SUB

    def spread_out(i, count):
        angles = got[pl.ds(i * (2 * cap), cap), :]
        vis = got[pl.ds(i * (2 * cap) + cap, cap), :]
        vis = vis - jnp.round(vis * (1.0 / DIGIT)) * DIGIT
        rows = pl.ds(count, cap)
        both = angles * (1.0 / (2.0 * math.pi))
        swapped = pltpu.roll(both, SUB, 1)
        turns_u[rows, :] = jnp.where(low_cap, both, swapped)
        turns_v[rows, :] = jnp.where(low_cap, swapped, both)
        both = vis * (1.0 / math.sqrt(SUB))
        swapped = pltpu.roll(both, SUB, 1)
        amp_a[rows, :] = jnp.where(low_cap, both, swapped)
        amp_b[rows, :] = jnp.where(low_cap, swapped, both)
        for k in range(cap):
            places[count + k] = cells[i * cap + k]
        return count + filled[i]

    count = lax.fori_loop(0, owners, spread_out, 0, unroll=8)
    for ref in (turns_u, turns_v, amp_a, amp_b):
        ref[pl.ds(count, 2 * group), :] = jnp.zeros((2 * group, LANES), jnp.float32)
    for k in range(2 * group):
        places[count + k] = 0
    pairs = jnp.maximum((count + 2 * group - 1) // (2 * group), 1)
    groups = 2 * pairs

    def offset_of(s, axis):
        return (places[s] >> (3 * DIGITS * axis)) & ((1 << (3 * DIGITS)) - 1)

    def clear(b, _):
        grid[pl.ds(b * grid_n, grid_n), :] = jnp.zeros((grid_n, LANES), grid.dtype)
        return 0

    lax.fori_loop(0, blocks + 1, clear, 0)

    def spread(ref, s):
        return jnp.broadcast_to(ref[pl.ds(s, 1), :], (ROWS, LANES))

    def find_bases(g, out):
        for i in range(group):
            s = g * group + i
            tu, tv = spread(turns_u, s), spread(turns_v, s)
            a, b = spread(amp_a, s), spread(amp_b, s)
            cs = sine_turns(tu * row_f + quarter)
            sc = pltpu.roll(cs, SUB, 1) * sign
            out[i, 0] = cs * a + sc * b
            out[i, 1] = sc * a - cs * b
            cs = sine_turns(tv * row_f + quarter)
            out[i, 2] = -(cs * sign)
            out[i, 3] = pltpu.roll(cs, SUB, 1)
            cs = sine_turns(jnp.where(upper, tu, tv) * eights + quarter)
            sc = pltpu.roll(cs, SUB, 1)
            out[i, 4] = jnp.where(low, cs, sc)
            out[i, 5] = jnp.where(low, sc, cs)

    def find_rows(source, left, right):
        for i in range(group):

            def line(k, j):
                return jnp.broadcast_to(source[i, k, j : j + 1, :], (ROWS, LANES))

            x, y = source[i, 0], source[i, 1]
            parts = [x]
            for j in range(middle):
                along, across = x * line(4, j), y * line(5, j)
                parts = [along - across] + parts
                if j + 1 < middle:
                    parts = parts + [along + across]
            left[i] = jnp.concatenate(parts, axis=0).astype(jnp.bfloat16)

            def keep(k, value_re, value_im):
                for place in (k, 2 * middle + k):
                    right[i, 0, place * ROWS : (place + 1) * ROWS, :] = value_re
                    right[i, 1, place * ROWS : (place + 1) * ROWS, :] = value_im

            x, y = source[i, 2], source[i, 3]
            keep(middle, x, y)
            for j in range(middle):
                wr, wi = line(4, middle + j), line(5, middle + j)
                xr, xi, yr, yi = x * wr, x * wi, y * wr, y * wi
                keep(middle - 1 - j, xr + yi, yr - xi)
                if j + 1 < middle:
                    keep(middle + 1 + j, xr - yi, yr + xi)

    def multiply(g, left, right, out):
        blank = jnp.zeros((SUB, LANES), jnp.bfloat16)
        for first_i in range(0, group, 2):
            halves = []
            for i in (first_i, first_i + 1):
                shift = offset_of(g * group + i, 1) & (SUB - 1)
                rows = pl.ds(SUB - shift, SUB)
                turned = jnp.concatenate([right[i, 0, rows, :], right[i, 1, rows, :]], axis=0)
                halves.append(turned.astype(jnp.bfloat16))
            upper_rows = jnp.concatenate([left[first_i], blank], axis=1)
            lower_rows = jnp.concatenate([blank, left[first_i + 1]], axis=1)
            both = lax.dot_general(
                jnp.concatenate([upper_rows, lower_rows], axis=0),
                jnp.concatenate(halves, axis=1),
                (((1,), (1,)), ((), ())),
                preferred_element_type=jnp.float32,
            )
            out[first_i] = both[:SUB]
            out[first_i + 1] = both[SUB:]

    cell = lax.broadcasted_iota(jnp.int32, (SUB, LANES), 1) & (SUB - 1)

    def add(g, formed):
        for i in range(group):
            s = g * group + i
            off_u, off_v = offset_of(s, 0), offset_of(s, 1)
            start = (off_v >> (SUB.bit_length() - 1)) * grid_n + off_u
            here = cell >= (off_v & (SUB - 1))
            places = [grid.at[pl.ds(start + side * grid_n, SUB), :] for side in range(2)]
            totals = [place[...] + formed[i] for place in places]
            pltpu.store(places[0], totals[0], mask=here)
            pltpu.store(places[1], totals[1], mask=~here)

    pieces[0][...] = jnp.zeros_like(pieces[0])
    lefts[1][...] = jnp.zeros_like(lefts[1])
    rights[1][...] = jnp.zeros_like(rights[1])
    find_bases(0, bases[0])

    def pair(p, _):
        for k in range(2):
            g = 2 * p + k
            add(jnp.maximum(g - 2, 0), pieces[k])
            multiply(jnp.maximum(g - 1, 0), lefts[1 - k], rights[1 - k], pieces[1 - k])
            find_rows(bases[k], lefts[k], rights[k])
            find_bases(jnp.minimum(g + 1, groups - 1), bases[1 - k])
        return 0

    lax.fori_loop(0, pairs, pair, 0)
    add(groups - 2, pieces[0])
    multiply(groups - 1, lefts[1], rights[1], pieces[1])
    add(groups - 1, pieces[1])

    for b in range(blocks):
        dense[:, b * LANES : (b + 1) * LANES] = grid[b * grid_n : (b + 1) * grid_n, :].astype(jnp.bfloat16)
    for copy in copies:
        copy.wait()


def form_grid(cells, filled, got, first, second):
    slots = got.shape[0] // 2
    grid_n = first.shape[0]
    blocks = grid_n // SUB
    group = math.gcd(slots // 2, GROUP)
    smem = pl.BlockSpec(memory_space=pltpu.SMEM)
    vmem = pl.BlockSpec(memory_space=pltpu.VMEM)
    hbm = pl.BlockSpec(memory_space=pltpu.HBM)
    line = pltpu.VMEM((slots + 2 * group, LANES), jnp.float32)
    stages = [
        pltpu.VMEM((group, 6, ROWS, LANES), jnp.float32),
        pltpu.VMEM((group, SUB, LANES), jnp.bfloat16),
        pltpu.VMEM((group, 2, 2 * SUB, LANES), jnp.float32),
        pltpu.VMEM((group, SUB, LANES), jnp.float32),
    ]
    return pl.pallas_call(
        grid_kernel,
        out_shape=[
            pltpu.VMEM((grid_n, 2 * grid_n), jnp.bfloat16),
            pltpu.VMEM(first.shape, jnp.bfloat16),
            pltpu.VMEM(second.shape, jnp.bfloat16),
        ],
        in_specs=[smem, smem, vmem, hbm, hbm],
        out_specs=[vmem] * 3,
        scratch_shapes=[
            line, line, line, line,
            pltpu.VMEM(((blocks + 1) * grid_n, LANES), jnp.float32),
            pltpu.SMEM((slots + 2 * group,), jnp.int32),
            pltpu.SemaphoreType.DMA((2,)),
            *(stage for stage in stages for _ in range(2)),
        ],
        compiler_params=pltpu.CompilerParams(vmem_limit_bytes=24 * 1024 * 1024),
        name="grid",
    )(
        cells,
        filled,
        got,
        pltpu.with_memory_space_constraint(first, pltpu.HBM),
        pltpu.with_memory_space_constraint(second, pltpu.HBM),
    )


def transform_rows(dense, first, second, start, end):
    grid_n = dense.shape[0]
    rows = end - start
    both = jnp.concatenate([first[start:end, :grid_n], first[start:end, grid_n:]], axis=0)
    both = jnp.dot(both, dense[...], preferred_element_type=jnp.float32)
    sign = jnp.where(lax.broadcasted_iota(jnp.int32, (rows, LANES), 1) < SUB, -1.0, 1.0)
    half = [
        both[:rows, at : at + LANES] + pltpu.roll(both[rows:, at : at + LANES], SUB, 1) * sign
        for at in range(0, 2 * grid_n, LANES)
    ]
    half = jnp.concatenate(half, axis=1).astype(jnp.bfloat16)
    return jnp.dot(half, second[...], preferred_element_type=jnp.float32)


def sent_rows_kernel(start, end, dense, first, second, *rest):
    image, send = rest[-2:]
    rows = transform_rows(dense, first, second, start, end)
    image[start:end, :] = rows
    send[...] = rows.astype(jnp.bfloat16)


def turn_rows(phase, turns, start, end):
    grid_n = phase.shape[1]
    part = phase[start:end, :] * (1.0 / (2.0 * math.pi))
    turns[start:end, :grid_n] = sine_turns(part + 0.25)
    turns[start:end, grid_n:] = sine_turns(part)


def other_rows_kernel(bounds, done, phase, dense, first, second, _, image, turns):
    for c, (start, end) in enumerate(zip(bounds, bounds[1:])):
        turn_rows(phase, turns, start, end)
        if c >= done:
            image[start:end, :] = transform_rows(dense, first, second, start, end)


def pinned(*arrays):
    return [pltpu.with_memory_space_constraint(x, pltpu.VMEM) for x in arrays]


def sent_rows(dense, first, second, start, end, image=None):
    grid_n = first.shape[0]
    vmem = pl.BlockSpec(memory_space=pltpu.VMEM)
    operands = [dense, first, second] + ([] if image is None else [image])
    return pl.pallas_call(
        functools.partial(sent_rows_kernel, start, end),
        out_shape=[
            pltpu.VMEM((grid_n, 2 * grid_n), jnp.float32),
            pltpu.VMEM((end - start, 2 * grid_n), jnp.bfloat16),
        ],
        in_specs=[vmem] * len(operands),
        out_specs=[vmem] * 2,
        input_output_aliases={} if image is None else {3: 0},
        compiler_params=pltpu.CompilerParams(vmem_limit_bytes=8 * 1024 * 1024),
        name="sent_rows",
    )(*pinned(*operands))


def other_rows(phase, dense, first, second, image, bounds, done):
    vmem = pl.BlockSpec(memory_space=pltpu.VMEM)
    return pl.pallas_call(
        functools.partial(other_rows_kernel, bounds, done),
        out_shape=[pltpu.VMEM(image.shape, jnp.float32), pltpu.VMEM(image.shape, jnp.float32)],
        in_specs=[vmem] * 5,
        out_specs=[vmem] * 2,
        input_output_aliases={4: 0},
        compiler_params=pltpu.CompilerParams(vmem_limit_bytes=8 * 1024 * 1024),
        name="other_rows",
    )(*pinned(phase, dense, first, second, image))


def dft_tables(grid_n):
    line = np.arange(grid_n)
    angle = (line[:, None] * line[None, :] % grid_n) * (2.0 * np.pi / grid_n)
    cos = np.cos(angle) / math.sqrt(grid_n)
    sin = np.sin(angle) / math.sqrt(grid_n)
    first = np.concatenate([cos, sin], axis=1)
    real = np.concatenate([cos, sin], axis=1).reshape(grid_n // SUB, SUB, 2 * grid_n)
    imag = np.concatenate([-sin, cos], axis=1).reshape(grid_n // SUB, SUB, 2 * grid_n)
    second = np.concatenate([real, imag], axis=1).reshape(2 * grid_n, 2 * grid_n)
    return first.astype(np.float32).astype(jnp.bfloat16), second.astype(np.float32).astype(jnp.bfloat16)


def send_up(part, hop):
    return lax.ppermute(part, "wa", [(hop - 1, hop)])


def turn_and_add(hop, start, incoming, image, turns, new_image, send=None):
    grid_n = image.shape[1] // 2
    rows = pl.ds(start, incoming.shape[0])
    re_cells, im_cells = pl.ds(0, grid_n), pl.ds(grid_n, grid_n)

    @pl.when(lax.axis_index("wa") == hop)
    def _():
        re = incoming[:, re_cells].astype(jnp.float32)
        im = incoming[:, im_cells].astype(jnp.float32)
        turn_re, turn_im = turns[rows, re_cells], turns[rows, im_cells]
        new_re = turn_re * re - turn_im * im + image[rows, re_cells]
        new_im = turn_re * im + turn_im * re + image[rows, im_cells]
        new_image[rows, re_cells] = new_re
        new_image[rows, im_cells] = new_im
        if send is not None:
            send[:, re_cells] = new_re.astype(jnp.bfloat16)
            send[:, im_cells] = new_im.astype(jnp.bfloat16)


def horner_kernel(hop, start, incoming, image, turns, send, new_image):
    turn_and_add(hop, start, incoming, image, turns, new_image, send)


def horner_step(hop, start, end, incoming, image, turns):
    vmem = pl.BlockSpec(memory_space=pltpu.VMEM)
    return pl.pallas_call(
        functools.partial(horner_kernel, hop, start),
        out_shape=[
            pltpu.VMEM((end - start, image.shape[1]), jnp.bfloat16),
            pltpu.VMEM(image.shape, jnp.float32),
        ],
        in_specs=[vmem] * 3,
        out_specs=[vmem] * 2,
        input_output_aliases={1: 1},
        compiler_params=pltpu.CompilerParams(vmem_limit_bytes=4 * 1024 * 1024),
        name="horner",
    )(*pinned(incoming, image, turns))


def last_kernel(hop, start, incoming, image, turns, *rest):
    new_image, result, sem = rest[-3:]
    turn_and_add(hop, start, incoming, image, turns, new_image)
    rows = pl.ds(start, incoming.shape[0])
    copy = pltpu.make_async_copy(new_image.at[rows, :], result.at[rows, :], sem)
    copy.start()
    copy.wait()


def last_step(hop, start, end, incoming, image, turns, result):
    vmem = pl.BlockSpec(memory_space=pltpu.VMEM)
    hbm = pl.BlockSpec(memory_space=pltpu.HBM)
    known = [] if result is None else [pltpu.with_memory_space_constraint(result, pltpu.HBM)]
    return pl.pallas_call(
        functools.partial(last_kernel, hop, start),
        out_shape=[pltpu.VMEM(image.shape, jnp.float32), pltpu.HBM(image.shape, jnp.float32)],
        in_specs=[vmem] * 3 + [hbm] * len(known),
        out_specs=[vmem, hbm],
        input_output_aliases={1: 0, **({3: 1} if known else {})},
        scratch_shapes=[pltpu.SemaphoreType.DMA],
        compiler_params=pltpu.CompilerParams(vmem_limit_bytes=4 * 1024 * 1024),
        name="last",
    )(*pinned(incoming, image, turns), *known)


def begin_kernel(start, image, send, _):
    @pl.when(lax.axis_index("wa") == 0)
    def _():
        send[...] = image[pl.ds(start, send.shape[0]), :].astype(jnp.bfloat16)


def begin_chain(start, end, image):
    vmem = pl.BlockSpec(memory_space=pltpu.VMEM)
    return pl.pallas_call(
        functools.partial(begin_kernel, start),
        out_shape=[
            pltpu.VMEM((end - start, image.shape[1]), jnp.bfloat16),
            pltpu.VMEM(image.shape, jnp.float32),
        ],
        in_specs=[vmem],
        out_specs=[vmem] * 2,
        input_output_aliases={0: 1},
        compiler_params=pltpu.CompilerParams(vmem_limit_bytes=4 * 1024 * 1024),
        name="begin",
    )(*pinned(image))


def on_device(visibilities, uv_angles, routes, offsets, pixel_phase):
    sub_count = visibilities.shape[0]
    count_vis = visibilities.shape[2]
    grid_n = pixel_phase.shape[1]
    planes = lax.axis_size("wa")
    owners = planes * lax.axis_size("facet")
    cap = max(2, (2 * sub_count + owners - 1) // owners)
    slots = owners * cap
    sent = pack(
        routes.T,
        offsets.T,
        uv_angles.transpose(1, 2, 0).reshape(2 * count_vis, sub_count),
        visibilities.transpose(1, 2, 0).reshape(2 * count_vis, sub_count),
        owners,
        cap,
    ).reshape(2 * slots, LANES)
    got = lax.all_to_all(sent, ("wa", "facet"), split_axis=0, concat_axis=0, tiled=True)
    digits = got.reshape(owners, 2, cap, LANES)[:, 1, :, : 2 * DIGITS + 1]
    digits = jnp.round(digits * (1.0 / DIGIT)).astype(jnp.int32)
    filled = jnp.sum(digits[:, :, 2 * DIGITS], axis=1)
    cells = digits[:, :, 0]
    for place in range(1, 2 * DIGITS):
        cells = cells + (digits[:, :, place] << (3 * place))
    first, second = (jnp.asarray(x) for x in dft_tables(grid_n))
    dense, first, second = form_grid(cells.reshape(slots), filled, got, first, second)

    units = grid_n // 16
    bounds = [0] + [16 * (units * sum(PARTS[: i + 1]) // sum(PARTS)) for i in range(len(PARTS))]
    count = len(PARTS)
    image, result, incoming = None, None, {}
    for c in range(EARLY):
        image, send = sent_rows(dense, first, second, bounds[c], bounds[c + 1], image)
        incoming[1, c] = send_up(send, 1)
    image, turns = other_rows(pixel_phase[0], dense, first, second, image, bounds, EARLY)

    def begin(c, image):
        if c < count:
            send, image = begin_chain(bounds[c], bounds[c + 1], image)
            incoming[1, c] = send_up(send, 1)
        return image

    for c in range(EARLY, AHEAD):
        image = begin(c, image)
    for beat in range(count + LAG * planes):
        for hop in range(1, planes):
            c = beat - LAG * (hop - 1)
            if 0 <= c < count:
                rows = bounds[c], bounds[c + 1]
                if hop + 1 < planes:
                    send, image = horner_step(hop, *rows, incoming[hop, c], image, turns)
                    incoming[hop + 1, c] = send_up(send, hop + 1)
                else:
                    image, result = last_step(hop, *rows, incoming[hop, c], image, turns, result)
                if hop == 1:
                    image = begin(c + AHEAD, image)
    return result.reshape(1, 1, grid_n, 2 * grid_n)


def solution(mesh):
    in_specs = (
        P(("wa", "facet"), None, None),
        P(("wa", "facet"), None, None),
        P(("wa", "facet"), None),
        P(("wa", "facet"), None),
        P("facet", None, None),
    )
    out_specs = P("wa", "facet", None, None)
    return jax.shard_map(
        on_device, mesh=mesh, in_specs=in_specs, out_specs=out_specs, check_vma=False
    )
```

profile of v0, /device:TPU:30, one launch (start us, length us, event | category | flops | bytes accessed | tf_op | source)
XLA Modules:
  0.0 67.7 jit_solution(11819633257464699380)
XLA Ops:
  0.0 1.3 %pack.1 = f32[32,2,8,128]{3,2,1,0:T(8,128)S(1)} custom-call(s32[1,128]{1,0:T(1,128)} %bitcast.24, s32[2,128]{1,0:T(2,128)} %bitcast.23, f32[128,128]{1,0:T(8,128)} %bitcast.21, bf16[128,128]{1,0:T(8,128)(2,1)} %bitcast.22), custom_call_target="tpu_custom_call" | custom-call | tf_op jit(solution)/shard_map/pack/pallas_call | solution.py:94
  1.3 12.8 %all_to_all.11 = f32[32,16,128]{2,1,0:T(8,128)S(1)} all-to-all(f32[32,16,128]{2,1,0:T(8,128)S(1)} %bitcast.20), channel_id=1, replica_groups=mesh['wa'=4,'facet'=8] {'wa','facet'}, dimensions={0} | all-to-all | bytes 524288 | tf_op jit(solution)/shard_map/all_to_all | solution.py:509
  14.4 4.5 %grid.1 = (bf16[512,1024]{1,0:T(8,128)(2,1)S(1)}, bf16[512,1024]{1,0:T(8,128)(2,1)S(1)}, bf16[1024,1024]{1,0:T(8,128)(2,1)S(1)}) custom-call(s32[256]{0:T(256)S(1)} %reshape.46.cells, s32[32]{0:T(128)S(1)} %get-tuple-element.93.filled, f32[512,128]{1,0:T(8,128)S(1)} %bitcast.18, bf16[512,1024]{1,0:T(8,128)(2,1)} %constant.18.clone.first_hbm, ...), custom_call_target="tpu_custom_call" | custom-call | tf_op jit(solution)/shard_map/grid/pallas_call | solution.py:294
  19.0 0.8 %sent_rows.3 = (f32[512,1024]{1,0:T(8,128)S(1)}, bf16[112,1024]{1,0:T(8,128)(2,1)S(1)}) custom-call(bf16[512,1024]{1,0:T(8,128)(2,1)S(1)} %get-tuple-element.49.dense, bf16[512,1024]{1,0:T(8,128)(2,1)S(1)} %get-tuple-element.50.first, bf16[1024,1024]{1,0:T(8,128)(2,1)S(1)} %get-tuple-element.51.second), custom_call_target="tpu_custom_call" | custom-call | tf_op jit(solution)/shard_map/sent_rows/pallas_call | solution.py:364
  19.8 0.7 collective-permute-start.1
  20.5 0.8 %sent_rows.4 = (f32[512,1024]{1,0:T(8,128)S(1)}, bf16[112,1024]{1,0:T(8,128)(2,1)S(1)}) custom-call(bf16[512,1024]{1,0:T(8,128)(2,1)S(1)} %get-tuple-element.49.dense, bf16[512,1024]{1,0:T(8,128)(2,1)S(1)} %get-tuple-element.50.first, bf16[1024,1024]{1,0:T(8,128)(2,1)S(1)} %get-tuple-element.51.second, ...), custom_call_target="tpu_custom_call", output_to_operand_aliasing={{0}: (3, {})} | custom-call | tf_op jit(solution)/shard_map/sent_rows/pallas_call | solution.py:364
  21.3 0.7 collective-permute-start
  22.0 0.8 %sent_rows.5 = (f32[512,1024]{1,0:T(8,128)S(1)}, bf16[112,1024]{1,0:T(8,128)(2,1)S(1)}) custom-call(bf16[512,1024]{1,0:T(8,128)(2,1)S(1)} %get-tuple-element.49.dense, bf16[512,1024]{1,0:T(8,128)(2,1)S(1)} %get-tuple-element.50.first, bf16[1024,1024]{1,0:T(8,128)(2,1)S(1)} %get-tuple-element.51.second, ...), custom_call_target="tpu_custom_call", output_to_operand_aliasing={{0}: (3, {})} | custom-call | tf_op jit(solution)/shard_map/sent_rows/pallas_call | solution.py:364
  22.8 0.7 collective-permute-start.6
  23.5 2.7 %other_rows.1 = (f32[512,1024]{1,0:T(8,128)S(1)}, f32[512,1024]{1,0:T(8,128)S(1)}) custom-call(f32[512,512]{1,0:T(8,128)S(1)} %bitcast.19, bf16[512,1024]{1,0:T(8,128)(2,1)S(1)} %get-tuple-element.49.dense, bf16[512,1024]{1,0:T(8,128)(2,1)S(1)} %get-tuple-element.50.first, ...), custom_call_target="tpu_custom_call", output_to_operand_aliasing={{0}: (4, {})} | custom-call | tf_op jit(solution)/shard_map/other_rows/pallas_call | solution.py:380
  26.3 0.7 collective-permute-start.5
  27.0 0.7 collective-permute-start.3
  27.7 0.7 collective-permute-start.4
  28.4 0.7 collective-permute-start.2
  29.1 0.7 collective-permute-start.11
  29.8 1.3 %collective-permute-start.10 = (bf16[112,1024]{1,0:T(8,128)(2,1)S(1)}, bf16[112,1024]{1,0:T(8,128)(2,1)S(1)}, u32[]{:S(2)}, u32[]{:S(2)}) collective-permute-start(bf16[112,1024]{1,0:T(8,128)(2,1)S(1)} %get-tuple-element.75), channel_id=1, source_target_pairs={{16,24},{17,25},{18,26},{19,27},{20,28},{21,29},{22,30},{23,31}} | collective-permute-start | bytes 688136 | tf_op jit(solution)/shard_map/ppermute | solution.py:404
  31.2 0.7 collective-permute-start.9
  31.9 1.3 %collective-permute-start.8 = (bf16[112,1024]{1,0:T(8,128)(2,1)S(1)}, bf16[112,1024]{1,0:T(8,128)(2,1)S(1)}, u32[]{:S(2)}, u32[]{:S(2)}) collective-permute-start(bf16[112,1024]{1,0:T(8,128)(2,1)S(1)} %get-tuple-element.73), channel_id=1, source_target_pairs={{16,24},{17,25},{18,26},{19,27},{20,28},{21,29},{22,30},{23,31}} | collective-permute-start | bytes 688136 | tf_op jit(solution)/shard_map/ppermute | solution.py:404
  33.2 0.7 collective-permute-start.7
  33.9 1.3 %collective-permute-start.14 = (bf16[112,1024]{1,0:T(8,128)(2,1)S(1)}, bf16[112,1024]{1,0:T(8,128)(2,1)S(1)}, u32[]{:S(2)}, u32[]{:S(2)}) collective-permute-start(bf16[112,1024]{1,0:T(8,128)(2,1)S(1)} %get-tuple-element.85), channel_id=1, source_target_pairs={{16,24},{17,25},{18,26},{19,27},{20,28},{21,29},{22,30},{23,31}} | collective-permute-start | bytes 688136 | tf_op jit(solution)/shard_map/ppermute | solution.py:404
  35.2 16.4 %collective-permute-done.10.incoming = bf16[112,1024]{1,0:T(8,128)(2,1)S(1)} collective-permute-done((bf16[112,1024]{1,0:T(8,128)(2,1)S(1)}, bf16[112,1024]{1,0:T(8,128)(2,1)S(1)}, u32[]{:S(2)}, u32[]{:S(2)}) %collective-permute-start.10) | collective-permute-done | bytes 229408 | tf_op jit(solution)/shard_map/ppermute | solution.py:404
  51.7 1.0 %last.5 = (f32[512,1024]{1,0:T(8,128)S(1)}, f32[512,1024]{1,0:T(8,128)}) custom-call(bf16[112,1024]{1,0:T(8,128)(2,1)S(1)} %collective-permute-done.10.incoming, f32[512,1024]{1,0:T(8,128)S(1)} %get-tuple-element.78.image, f32[512,1024]{1,0:T(8,128)S(1)} %get-tuple-element.58.turns), custom_call_target="tpu_custom_call", output_to_operand_aliasing={{0}: (1, {})} | custom-call | tf_op jit(solution)/shard_map/last/pallas_call | solution.py:459
  52.7 1.3 %collective-permute-start.13 = (bf16[96,1024]{1,0:T(8,128)(2,1)S(1)}, bf16[96,1024]{1,0:T(8,128)(2,1)S(1)}, u32[]{:S(2)}, u32[]{:S(2)}) collective-permute-start(bf16[96,1024]{1,0:T(8,128)(2,1)S(1)} %get-tuple-element.84), channel_id=1, source_target_pairs={{16,24},{17,25},{18,26},{19,27},{20,28},{21,29},{22,30},{23,31}} | collective-permute-start | bytes 589832 | tf_op jit(solution)/shard_map/ppermute | solution.py:404
  54.0 3.3 %collective-permute-done.8.incoming = bf16[112,1024]{1,0:T(8,128)(2,1)S(1)} collective-permute-done((bf16[112,1024]{1,0:T(8,128)(2,1)S(1)}, bf16[112,1024]{1,0:T(8,128)(2,1)S(1)}, u32[]{:S(2)}, u32[]{:S(2)}) %collective-permute-start.8) | collective-permute-done | bytes 229408 | tf_op jit(solution)/shard_map/ppermute | solution.py:404
  57.3 1.0 %last.6 = (f32[512,1024]{1,0:T(8,128)S(1)}, f32[512,1024]{1,0:T(8,128)}) custom-call(bf16[112,1024]{1,0:T(8,128)(2,1)S(1)} %collective-permute-done.8.incoming, f32[512,1024]{1,0:T(8,128)S(1)} %get-tuple-element.80.image, f32[512,1024]{1,0:T(8,128)S(1)} %get-tuple-element.58.turns, ...), custom_call_target="tpu_custom_call", output_to_operand_aliasing={{0}: (1, {}), {1}: (3, {})} | custom-call | tf_op jit(solution)/shard_map/last/pallas_call | solution.py:459
  58.3 1.3 %collective-permute-start.12 = (bf16[80,1024]{1,0:T(8,128)(2,1)S(1)}, bf16[80,1024]{1,0:T(8,128)(2,1)S(1)}, u32[]{:S(2)}, u32[]{:S(2)}) collective-permute-start(bf16[80,1024]{1,0:T(8,128)(2,1)S(1)} %get-tuple-element.83), channel_id=1, source_target_pairs={{16,24},{17,25},{18,26},{19,27},{20,28},{21,29},{22,30},{23,31}} | collective-permute-start | bytes 491528 | tf_op jit(solution)/shard_map/ppermute | solution.py:404
  59.6 3.3 %collective-permute-done.14.incoming = bf16[112,1024]{1,0:T(8,128)(2,1)S(1)} collective-permute-done((bf16[112,1024]{1,0:T(8,128)(2,1)S(1)}, bf16[112,1024]{1,0:T(8,128)(2,1)S(1)}, u32[]{:S(2)}, u32[]{:S(2)}) %collective-permute-start.14) | collective-permute-done | bytes 229408 | tf_op jit(solution)/shard_map/ppermute | solution.py:404
  63.0 1.0 %last.7 = (f32[512,1024]{1,0:T(8,128)S(1)}, f32[512,1024]{1,0:T(8,128)}) custom-call(bf16[112,1024]{1,0:T(8,128)(2,1)S(1)} %collective-permute-done.14.incoming, f32[512,1024]{1,0:T(8,128)S(1)} %get-tuple-element.86.image, f32[512,1024]{1,0:T(8,128)S(1)} %get-tuple-element.58.turns, ...), custom_call_target="tpu_custom_call", output_to_operand_aliasing={{0}: (1, {}), {1}: (3, {})} | custom-call | tf_op jit(solution)/shard_map/last/pallas_call | solution.py:459
  64.0 1.1 %collective-permute-done.13.incoming = bf16[96,1024]{1,0:T(8,128)(2,1)S(1)} collective-permute-done((bf16[96,1024]{1,0:T(8,128)(2,1)S(1)}, bf16[96,1024]{1,0:T(8,128)(2,1)S(1)}, u32[]{:S(2)}, u32[]{:S(2)}) %collective-permute-start.13) | collective-permute-done | bytes 196640 | tf_op jit(solution)/shard_map/ppermute | solution.py:404
  65.1 0.9 %last.8 = (f32[512,1024]{1,0:T(8,128)S(1)}, f32[512,1024]{1,0:T(8,128)}) custom-call(bf16[96,1024]{1,0:T(8,128)(2,1)S(1)} %collective-permute-done.13.incoming, f32[512,1024]{1,0:T(8,128)S(1)} %get-tuple-element.88.image, f32[512,1024]{1,0:T(8,128)S(1)} %get-tuple-element.58.turns, ...), custom_call_target="tpu_custom_call", output_to_operand_aliasing={{0}: (1, {}), {1}: (3, {})} | custom-call | tf_op jit(solution)/shard_map/last/pallas_call | solution.py:459
  66.0 0.8 %collective-permute-done.12.incoming = bf16[80,1024]{1,0:T(8,128)(2,1)S(1)} collective-permute-done((bf16[80,1024]{1,0:T(8,128)(2,1)S(1)}, bf16[80,1024]{1,0:T(8,128)(2,1)S(1)}, u32[]{:S(2)}, u32[]{:S(2)}) %collective-permute-start.12) | collective-permute-done | bytes 163872 | tf_op jit(solution)/shard_map/ppermute | solution.py:404
  66.8 0.9 %last.9 = (f32[512,1024]{1,0:T(8,128)S(1)}, f32[512,1024]{1,0:T(8,128)}) custom-call(bf16[80,1024]{1,0:T(8,128)(2,1)S(1)} %collective-permute-done.12.incoming, f32[512,1024]{1,0:T(8,128)S(1)} %get-tuple-element.90.image, f32[512,1024]{1,0:T(8,128)S(1)} %get-tuple-element.58.turns, ...), custom_call_target="tpu_custom_call", output_to_operand_aliasing={{0}: (1, {}), {1}: (3, {})} | custom-call | tf_op jit(solution)/shard_map/last/pallas_call | solution.py:459
  (30 shorter events, 0.6 us)
Async XLA Ops:
  19.8 6.5 %collective-permute-start.1 = (bf16[112,1024]{1,0:T(8,128)(2,1)S(1)}, bf16[112,1024]{1,0:T(8,128)(2,1)S(1)}, u32[]{:S(2)}, u32[]{:S(2)}) collective-permute-start(bf16[112,1024]{1,0:T(8,128)(2,1)S(1)} %get-tuple-element.54), channel_id=1, source_target_pairs={{0,8},{1,9},{2,10},{3,11},{4,12},{5,13},{6,14},{7,15}} | collective-permute-start | bytes 688136 | tf_op jit(solution)/shard_map/ppermute | solution.py:404
  21.3 5.7 %collective-permute-start = (bf16[112,1024]{1,0:T(8,128)(2,1)S(1)}, bf16[112,1024]{1,0:T(8,128)(2,1)S(1)}, u32[]{:S(2)}, u32[]{:S(2)}) collective-permute-start(bf16[112,1024]{1,0:T(8,128)(2,1)S(1)} %get-tuple-element.53), channel_id=1, source_target_pairs={{0,8},{1,9},{2,10},{3,11},{4,12},{5,13},{6,14},{7,15}} | collective-permute-start | bytes 688136 | tf_op jit(solution)/shard_map/ppermute | solution.py:404
  22.0 1.5 %copy-start = (f32[1,512,512]{2,1,0:T(8,128)S(1)}, f32[1,512,512]{2,1,0:T(8,128)}, u32[]{:S(2)}) copy-start(f32[1,512,512]{2,1,0:T(8,128)} %param.11) | copy-start | bytes 3145732
  22.8 6.3 %collective-permute-start.6 = (bf16[112,1024]{1,0:T(8,128)(2,1)S(1)}, bf16[112,1024]{1,0:T(8,128)(2,1)S(1)}, u32[]{:S(2)}, u32[]{:S(2)}) collective-permute-start(bf16[112,1024]{1,0:T(8,128)(2,1)S(1)} %get-tuple-element.66), channel_id=1, source_target_pairs={{0,8},{1,9},{2,10},{3,11},{4,12},{5,13},{6,14},{7,15}} | collective-permute-start | bytes 688136 | tf_op jit(solution)/shard_map/ppermute | solution.py:404
  26.3 3.5 %collective-permute-start.5 = (bf16[112,1024]{1,0:T(8,128)(2,1)S(1)}, bf16[112,1024]{1,0:T(8,128)(2,1)S(1)}, u32[]{:S(2)}, u32[]{:S(2)}) collective-permute-start(bf16[112,1024]{1,0:T(8,128)(2,1)S(1)} %get-tuple-element.65), channel_id=1, source_target_pairs={{8,16},{9,17},{10,18},{11,19},{12,20},{13,21},{14,22},{15,23}} | collective-permute-start | bytes 688136 | tf_op jit(solution)/shard_map/ppermute | solution.py:404
  27.0 4.8 %collective-permute-start.3 = (bf16[112,1024]{1,0:T(8,128)(2,1)S(1)}, bf16[112,1024]{1,0:T(8,128)(2,1)S(1)}, u32[]{:S(2)}, u32[]{:S(2)}) collective-permute-start(bf16[112,1024]{1,0:T(8,128)(2,1)S(1)} %get-tuple-element.63), channel_id=1, source_target_pairs={{8,16},{9,17},{10,18},{11,19},{12,20},{13,21},{14,22},{15,23}} | collective-permute-start | bytes 688136 | tf_op jit(solution)/shard_map/ppermute | solution.py:404
  27.7 3.4 %collective-permute-start.4 = (bf16[96,1024]{1,0:T(8,128)(2,1)S(1)}, bf16[96,1024]{1,0:T(8,128)(2,1)S(1)}, u32[]{:S(2)}, u32[]{:S(2)}) collective-permute-start(bf16[96,1024]{1,0:T(8,128)(2,1)S(1)} %get-tuple-element.64), channel_id=1, source_target_pairs={{0,8},{1,9},{2,10},{3,11},{4,12},{5,13},{6,14},{7,15}} | collective-permute-start | bytes 589832 | tf_op jit(solution)/shard_map/ppermute | solution.py:404
  28.4 4.8 %collective-permute-start.2 = (bf16[80,1024]{1,0:T(8,128)(2,1)S(1)}, bf16[80,1024]{1,0:T(8,128)(2,1)S(1)}, u32[]{:S(2)}, u32[]{:S(2)}) collective-permute-start(bf16[80,1024]{1,0:T(8,128)(2,1)S(1)} %get-tuple-element.62), channel_id=1, source_target_pairs={{0,8},{1,9},{2,10},{3,11},{4,12},{5,13},{6,14},{7,15}} | collective-permute-start | bytes 491528 | tf_op jit(solution)/shard_map/ppermute | solution.py:404
  29.1 4.8 %collective-permute-start.11 = (bf16[112,1024]{1,0:T(8,128)(2,1)S(1)}, bf16[112,1024]{1,0:T(8,128)(2,1)S(1)}, u32[]{:S(2)}, u32[]{:S(2)}) collective-permute-start(bf16[112,1024]{1,0:T(8,128)(2,1)S(1)} %get-tuple-element.76), channel_id=1, source_target_pairs={{8,16},{9,17},{10,18},{11,19},{12,20},{13,21},{14,22},{15,23}} | collective-permute-start | bytes 688136 | tf_op jit(solution)/shard_map/ppermute | solution.py:404
  29.8 21.9 %collective-permute-start.10 = (bf16[112,1024]{1,0:T(8,128)(2,1)S(1)}, bf16[112,1024]{1,0:T(8,128)(2,1)S(1)}, u32[]{:S(2)}, u32[]{:S(2)}) collective-permute-start(bf16[112,1024]{1,0:T(8,128)(2,1)S(1)} %get-tuple-element.75), channel_id=1, source_target_pairs={{16,24},{17,25},{18,26},{19,27},{20,28},{21,29},{22,30},{23,31}} | collective-permute-start | bytes 688136 | tf_op jit(solution)/shard_map/ppermute | solution.py:404
  31.2 21.5 %collective-permute-start.9 = (bf16[96,1024]{1,0:T(8,128)(2,1)S(1)}, bf16[96,1024]{1,0:T(8,128)(2,1)S(1)}, u32[]{:S(2)}, u32[]{:S(2)}) collective-permute-start(bf16[96,1024]{1,0:T(8,128)(2,1)S(1)} %get-tuple-element.74), channel_id=1, source_target_pairs={{8,16},{9,17},{10,18},{11,19},{12,20},{13,21},{14,22},{15,23}} | collective-permute-start | bytes 589832 | tf_op jit(solution)/shard_map/ppermute | solution.py:404
  31.9 25.4 %collective-permute-start.8 = (bf16[112,1024]{1,0:T(8,128)(2,1)S(1)}, bf16[112,1024]{1,0:T(8,128)(2,1)S(1)}, u32[]{:S(2)}, u32[]{:S(2)}) collective-permute-start(bf16[112,1024]{1,0:T(8,128)(2,1)S(1)} %get-tuple-element.73), channel_id=1, source_target_pairs={{16,24},{17,25},{18,26},{19,27},{20,28},{21,29},{22,30},{23,31}} | collective-permute-start | bytes 688136 | tf_op jit(solution)/shard_map/ppermute | solution.py:404
  33.2 25.1 %collective-permute-start.7 = (bf16[80,1024]{1,0:T(8,128)(2,1)S(1)}, bf16[80,1024]{1,0:T(8,128)(2,1)S(1)}, u32[]{:S(2)}, u32[]{:S(2)}) collective-permute-start(bf16[80,1024]{1,0:T(8,128)(2,1)S(1)} %get-tuple-element.72), channel_id=1, source_target_pairs={{8,16},{9,17},{10,18},{11,19},{12,20},{13,21},{14,22},{15,23}} | collective-permute-start | bytes 491528 | tf_op jit(solution)/shard_map/ppermute | solution.py:404
  33.9 29.0 %collective-permute-start.14 = (bf16[112,1024]{1,0:T(8,128)(2,1)S(1)}, bf16[112,1024]{1,0:T(8,128)(2,1)S(1)}, u32[]{:S(2)}, u32[]{:S(2)}) collective-permute-start(bf16[112,1024]{1,0:T(8,128)(2,1)S(1)} %get-tuple-element.85), channel_id=1, source_target_pairs={{16,24},{17,25},{18,26},{19,27},{20,28},{21,29},{22,30},{23,31}} | collective-permute-start | bytes 688136 | tf_op jit(solution)/shard_map/ppermute | solution.py:404
  52.7 12.3 %collective-permute-start.13 = (bf16[96,1024]{1,0:T(8,128)(2,1)S(1)}, bf16[96,1024]{1,0:T(8,128)(2,1)S(1)}, u32[]{:S(2)}, u32[]{:S(2)}) collective-permute-start(bf16[96,1024]{1,0:T(8,128)(2,1)S(1)} %get-tuple-element.84), channel_id=1, source_target_pairs={{16,24},{17,25},{18,26},{19,27},{20,28},{21,29},{22,30},{23,31}} | collective-permute-start | bytes 589832 | tf_op jit(solution)/shard_map/ppermute | solution.py:404
  58.3 8.5 %collective-permute-start.12 = (bf16[80,1024]{1,0:T(8,128)(2,1)S(1)}, bf16[80,1024]{1,0:T(8,128)(2,1)S(1)}, u32[]{:S(2)}, u32[]{:S(2)}) collective-permute-start(bf16[80,1024]{1,0:T(8,128)(2,1)S(1)} %get-tuple-element.83), channel_id=1, source_target_pairs={{16,24},{17,25},{18,26},{19,27},{20,28},{21,29},{22,30},{23,31}} | collective-permute-start | bytes 491528 | tf_op jit(solution)/shard_map/ppermute | solution.py:404
where the time goes:
time: 67.9 us; the launch traced here: 67.7 us
  waiting for transfers between devices  25 us (37%)
  Pallas kernels  16 us (24%)
  starting transfers between devices  13.2 us (19%)
  blocking collectives  12.8 us (19%)
    ppermute x15, waiting for transfers between devices, send_up(): return lax.ppermute(part, 'wa', [(hop - 1, hop)])  25 us
    ppermute x15, starting transfers between devices, send_up(): return lax.ppermute(part, 'wa', [(hop - 1, hop)])  13.2 us
    all_to_all x1, blocking collectives, on_device(): lax.all_to_all(sent, ('wa', 'facet'), split_axis=0, concat_axis=0, tiled=...  12.8 us
    pallas_call x5, Pallas kernels, last_step(): pl.pallas_call(functools.partial(last_kernel, hop, start), out_shape=[plt...  4.79 us
    pallas_call x1, Pallas kernels, form_grid(): pl.pallas_call(grid_kernel, out_shape=[pltpu.VMEM((grid_n, 2 * grid_n), j...  4.5 us
    pallas_call x1, Pallas kernels, other_rows(): pl.pallas_call(functools.partial(other_rows_kernel, bounds, done), out_sh...  2.72 us
    pallas_call x3, Pallas kernels, sent_rows(): pl.pallas_call(functools.partial(sent_rows_kernel, start, end), out_shape...  2.48 us
  transfers between devices with their start and end apart: 15, of which 5 were waited for; matrix products, arithmetic and copies ran while one was open for 0% of the time, Pallas kernels for 13%

commit v1 on v0

--- a/solution.py
+++ b/solution.py
@@ -13,7 +13,7 @@
 LANES = 128
 ROWS = 8
 GROUP = 8
-PARTS = (7, 7, 7, 6, 5)
+PARTS = (7, 7, 7, 7, 4)
 EARLY = 3
 AHEAD = 3
 LAG = 2
@@ -106,12 +106,11 @@
 
 
 def grid_kernel(
-    cells, filled, got, first_hbm, second_hbm, dense, first, second,
+    cap, cells, got, first_hbm, second_hbm, dense, first, second,
     turns_u, turns_v, amp_a, amp_b, grid, places, sems, *stages,
 ):
     slots = got.shape[0] // 2
-    owners = filled.shape[0]
-    cap = slots // owners
+    owners = slots // cap
     grid_n = dense.shape[0]
     blocks = grid_n // SUB
     group = stages[0].shape[0]
@@ -150,7 +149,7 @@
         amp_b[rows, :] = jnp.where(low_cap, swapped, both)
         for k in range(cap):
             places[count + k] = cells[i * cap + k]
-        return count + filled[i]
+        return count + cells[slots + i]
 
     count = lax.fori_loop(0, owners, spread_out, 0, unroll=8)
     for ref in (turns_u, turns_v, amp_a, amp_b):
@@ -276,7 +275,7 @@
         copy.wait()
 
 
-def form_grid(cells, filled, got, first, second):
+def form_grid(cells, got, first, second, cap):
     slots = got.shape[0] // 2
     grid_n = first.shape[0]
     blocks = grid_n // SUB
@@ -292,13 +291,13 @@
         pltpu.VMEM((group, SUB, LANES), jnp.float32),
     ]
     return pl.pallas_call(
-        grid_kernel,
+        functools.partial(grid_kernel, cap),
         out_shape=[
             pltpu.VMEM((grid_n, 2 * grid_n), jnp.bfloat16),
             pltpu.VMEM(first.shape, jnp.bfloat16),
             pltpu.VMEM(second.shape, jnp.bfloat16),
         ],
-        in_specs=[smem, smem, vmem, hbm, hbm],
+        in_specs=[smem, vmem, hbm, hbm],
         out_specs=[vmem] * 3,
         scratch_shapes=[
             line, line, line, line,
@@ -311,7 +310,6 @@
         name="grid",
     )(
         cells,
-        filled,
         got,
         pltpu.with_memory_space_constraint(first, pltpu.HBM),
         pltpu.with_memory_space_constraint(second, pltpu.HBM),
@@ -513,8 +511,9 @@
     cells = digits[:, :, 0]
     for place in range(1, 2 * DIGITS):
         cells = cells + (digits[:, :, place] << (3 * place))
+    cells = jnp.concatenate([cells.reshape(slots), filled])
     first, second = (jnp.asarray(x) for x in dft_tables(grid_n))
-    dense, first, second = form_grid(cells.reshape(slots), filled, got, first, second)
+    dense, first, second = form_grid(cells, got, first, second, cap)
 
     units = grid_n // 16
     bounds = [0] + [16 * (units * sum(PARTS[: i + 1]) // sum(PARTS)) for i in range(len(PARTS))]

time: 67.9 us -> 68.5 us (level); the launches traced: 67.7 us -> 67.3 us
  waiting for transfers between devices: 25 us -> 23.5 us
  Pallas kernels: 16 us -> 17.1 us
    ppermute x15, waiting for transfers between devices: 25 us -> 23.5 us  [send_up(): return lax.ppermute(part, 'wa', [(hop - 1, hop)])]
    pallas_call x1, Pallas kernels: 4.5 us -> 5.52 us  [form_grid(): pl.pallas_call(functools.partial(grid_kernel, cap), out_shape=[pltpu.VMEM...]
where the time goes in v1:
time: 68.5 us; the launch traced here: 67.3 us
  waiting for transfers between devices  23.5 us (34%)
  Pallas kernels  17.1 us (25%)
  starting transfers between devices  13.2 us (19%)
  blocking collectives  12.8 us (19%)
    ppermute x15, waiting for transfers between devices, send_up(): return lax.ppermute(part, 'wa', [(hop - 1, hop)])  23.5 us
    ppermute x15, starting transfers between devices, send_up(): return lax.ppermute(part, 'wa', [(hop - 1, hop)])  13.2 us
    all_to_all x1, blocking collectives, on_device(): lax.all_to_all(sent, ('wa', 'facet'), split_axis=0, concat_axis=0, tiled=...  12.8 us
    pallas_call x1, Pallas kernels, form_grid(): pl.pallas_call(functools.partial(grid_kernel, cap), out_shape=[pltpu.VMEM...  5.52 us
    pallas_call x5, Pallas kernels, last_step(): pl.pallas_call(functools.partial(last_kernel, hop, start), out_shape=[plt...  4.78 us
    pallas_call x1, Pallas kernels, other_rows(): pl.pallas_call(functools.partial(other_rows_kernel, bounds, done), out_sh...  2.79 us
    pallas_call x3, Pallas kernels, sent_rows(): pl.pallas_call(functools.partial(sent_rows_kernel, start, end), out_shape...  2.54 us
  transfers between devices with their start and end apart: 15, of which 5 were waited for; matrix products, arithmetic and copies ran while one was open for 0% of the time, Pallas kernels for 13%

profile of v1, /device:TPU:30, one launch (start us, length us, event | category | flops | bytes accessed | tf_op | source)
XLA Modules:
  0.0 67.3 jit_solution(15196731692624450608)
XLA Ops:
  0.0 1.3 %pack.1 = f32[32,2,8,128]{3,2,1,0:T(8,128)S(1)} custom-call(s32[1,128]{1,0:T(1,128)} %bitcast.24, s32[2,128]{1,0:T(2,128)} %bitcast.23, f32[128,128]{1,0:T(8,128)} %bitcast.21, bf16[128,128]{1,0:T(8,128)(2,1)} %bitcast.22), custom_call_target="tpu_custom_call" | custom-call | tf_op jit(solution)/shard_map/pack/pallas_call | solution.py:94
  1.3 12.8 %all_to_all.11 = f32[32,16,128]{2,1,0:T(8,128)S(1)} all-to-all(f32[32,16,128]{2,1,0:T(8,128)S(1)} %bitcast.20), channel_id=1, replica_groups=mesh['wa'=4,'facet'=8] {'wa','facet'}, dimensions={0} | all-to-all | bytes 524288 | tf_op jit(solution)/shard_map/all_to_all | solution.py:507
  14.5 5.5 %grid.1 = (bf16[512,1024]{1,0:T(8,128)(2,1)S(1)}, bf16[512,1024]{1,0:T(8,128)(2,1)S(1)}, bf16[1024,1024]{1,0:T(8,128)(2,1)S(1)}) custom-call(s32[288]{0:T(512)S(1)} %pad_add_fusion.cells, f32[512,128]{1,0:T(8,128)S(1)} %bitcast.18, bf16[512,1024]{1,0:T(8,128)(2,1)} %constant.18.clone.first_hbm, bf16[1024,1024]{1,0:T(8,128)(2,1)} %constant.19.clone.second_hbm), custom_call_target="tpu_custom_call" | custom-call | tf_op jit(solution)/shard_map/grid/pallas_call | solution.py:293
  20.0 0.9 %sent_rows.3 = (f32[512,1024]{1,0:T(8,128)S(1)}, bf16[112,1024]{1,0:T(8,128)(2,1)S(1)}) custom-call(bf16[512,1024]{1,0:T(8,128)(2,1)S(1)} %get-tuple-element.49.dense, bf16[512,1024]{1,0:T(8,128)(2,1)S(1)} %get-tuple-element.50.first, bf16[1024,1024]{1,0:T(8,128)(2,1)S(1)} %get-tuple-element.51.second), custom_call_target="tpu_custom_call" | custom-call | tf_op jit(solution)/shard_map/sent_rows/pallas_call | solution.py:362
  20.8 0.7 %collective-permute-start.1 = (bf16[112,1024]{1,0:T(8,128)(2,1)S(1)}, bf16[112,1024]{1,0:T(8,128)(2,1)S(1)}, u32[]{:S(2)}, u32[]{:S(2)}) collective-permute-start(bf16[112,1024]{1,0:T(8,128)(2,1)S(1)} %get-tuple-element.54), channel_id=1, source_target_pairs={{0,8},{1,9},{2,10},{3,11},{4,12},{5,13},{6,14},{7,15}} | collective-permute-start | bytes 688136 | tf_op jit(solution)/shard_map/ppermute | solution.py:402
  21.5 0.8 %sent_rows.4 = (f32[512,1024]{1,0:T(8,128)S(1)}, bf16[112,1024]{1,0:T(8,128)(2,1)S(1)}) custom-call(bf16[512,1024]{1,0:T(8,128)(2,1)S(1)} %get-tuple-element.49.dense, bf16[512,1024]{1,0:T(8,128)(2,1)S(1)} %get-tuple-element.50.first, bf16[1024,1024]{1,0:T(8,128)(2,1)S(1)} %get-tuple-element.51.second, ...), custom_call_target="tpu_custom_call", output_to_operand_aliasing={{0}: (3, {})} | custom-call | tf_op jit(solution)/shard_map/sent_rows/pallas_call | solution.py:362
  22.4 0.7 %collective-permute-start = (bf16[112,1024]{1,0:T(8,128)(2,1)S(1)}, bf16[112,1024]{1,0:T(8,128)(2,1)S(1)}, u32[]{:S(2)}, u32[]{:S(2)}) collective-permute-start(bf16[112,1024]{1,0:T(8,128)(2,1)S(1)} %get-tuple-element.53), channel_id=1, source_target_pairs={{0,8},{1,9},{2,10},{3,11},{4,12},{5,13},{6,14},{7,15}} | collective-permute-start | bytes 688136 | tf_op jit(solution)/shard_map/ppermute | solution.py:402
  23.1 0.8 %sent_rows.5 = (f32[512,1024]{1,0:T(8,128)S(1)}, bf16[112,1024]{1,0:T(8,128)(2,1)S(1)}) custom-call(bf16[512,1024]{1,0:T(8,128)(2,1)S(1)} %get-tuple-element.49.dense, bf16[512,1024]{1,0:T(8,128)(2,1)S(1)} %get-tuple-element.50.first, bf16[1024,1024]{1,0:T(8,128)(2,1)S(1)} %get-tuple-element.51.second, ...), custom_call_target="tpu_custom_call", output_to_operand_aliasing={{0}: (3, {})} | custom-call | tf_op jit(solution)/shard_map/sent_rows/pallas_call | solution.py:362
  23.9 0.7 %collective-permute-start.6 = (bf16[112,1024]{1,0:T(8,128)(2,1)S(1)}, bf16[112,1024]{1,0:T(8,128)(2,1)S(1)}, u32[]{:S(2)}, u32[]{:S(2)}) collective-permute-start(bf16[112,1024]{1,0:T(8,128)(2,1)S(1)} %get-tuple-element.66), channel_id=1, source_target_pairs={{0,8},{1,9},{2,10},{3,11},{4,12},{5,13},{6,14},{7,15}} | collective-permute-start | bytes 688136 | tf_op jit(solution)/shard_map/ppermute | solution.py:402
  24.6 2.8 %other_rows.1 = (f32[512,1024]{1,0:T(8,128)S(1)}, f32[512,1024]{1,0:T(8,128)S(1)}) custom-call(f32[512,512]{1,0:T(8,128)S(1)} %bitcast.19, bf16[512,1024]{1,0:T(8,128)(2,1)S(1)} %get-tuple-element.49.dense, bf16[512,1024]{1,0:T(8,128)(2,1)S(1)} %get-tuple-element.50.first, ...), custom_call_target="tpu_custom_call", output_to_operand_aliasing={{0}: (4, {})} | custom-call | tf_op jit(solution)/shard_map/other_rows/pallas_call | solution.py:378
  27.5 0.7 %collective-permute-start.5 = (bf16[112,1024]{1,0:T(8,128)(2,1)S(1)}, bf16[112,1024]{1,0:T(8,128)(2,1)S(1)}, u32[]{:S(2)}, u32[]{:S(2)}) collective-permute-start(bf16[112,1024]{1,0:T(8,128)(2,1)S(1)} %get-tuple-element.65), channel_id=1, source_target_pairs={{8,16},{9,17},{10,18},{11,19},{12,20},{13,21},{14,22},{15,23}} | collective-permute-start | bytes 688136 | tf_op jit(solution)/shard_map/ppermute | solution.py:402
  28.2 0.7 %collective-permute-start.4 = (bf16[112,1024]{1,0:T(8,128)(2,1)S(1)}, bf16[112,1024]{1,0:T(8,128)(2,1)S(1)}, u32[]{:S(2)}, u32[]{:S(2)}) collective-permute-start(bf16[112,1024]{1,0:T(8,128)(2,1)S(1)} %get-tuple-element.64), channel_id=1, source_target_pairs={{0,8},{1,9},{2,10},{3,11},{4,12},{5,13},{6,14},{7,15}} | collective-permute-start | bytes 688136 | tf_op jit(solution)/shard_map/ppermute | solution.py:402
  28.9 0.7 %collective-permute-start.3 = (bf16[112,1024]{1,0:T(8,128)(2,1)S(1)}, bf16[112,1024]{1,0:T(8,128)(2,1)S(1)}, u32[]{:S(2)}, u32[]{:S(2)}) collective-permute-start(bf16[112,1024]{1,0:T(8,128)(2,1)S(1)} %get-tuple-element.63), channel_id=1, source_target_pairs={{8,16},{9,17},{10,18},{11,19},{12,20},{13,21},{14,22},{15,23}} | collective-permute-start | bytes 688136 | tf_op jit(solution)/shard_map/ppermute | solution.py:402
  29.6 0.7 %collective-permute-start.11 = (bf16[112,1024]{1,0:T(8,128)(2,1)S(1)}, bf16[112,1024]{1,0:T(8,128)(2,1)S(1)}, u32[]{:S(2)}, u32[]{:S(2)}) collective-permute-start(bf16[112,1024]{1,0:T(8,128)(2,1)S(1)} %get-tuple-element.76), channel_id=1, source_target_pairs={{8,16},{9,17},{10,18},{11,19},{12,20},{13,21},{14,22},{15,23}} | collective-permute-start | bytes 688136 | tf_op jit(solution)/shard_map/ppermute | solution.py:402
  30.3 1.3 %collective-permute-start.10 = (bf16[112,1024]{1,0:T(8,128)(2,1)S(1)}, bf16[112,1024]{1,0:T(8,128)(2,1)S(1)}, u32[]{:S(2)}, u32[]{:S(2)}) collective-permute-start(bf16[112,1024]{1,0:T(8,128)(2,1)S(1)} %get-tuple-element.75), channel_id=1, source_target_pairs={{16,24},{17,25},{18,26},{19,27},{20,28},{21,29},{22,30},{23,31}} | collective-permute-start | bytes 688136 | tf_op jit(solution)/shard_map/ppermute | solution.py:402
  31.7 0.7 %collective-permute-start.9 = (bf16[112,1024]{1,0:T(8,128)(2,1)S(1)}, bf16[112,1024]{1,0:T(8,128)(2,1)S(1)}, u32[]{:S(2)}, u32[]{:S(2)}) collective-permute-start(bf16[112,1024]{1,0:T(8,128)(2,1)S(1)} %get-tuple-element.74), channel_id=1, source_target_pairs={{8,16},{9,17},{10,18},{11,19},{12,20},{13,21},{14,22},{15,23}} | collective-permute-start | bytes 688136 | tf_op jit(solution)/shard_map/ppermute | solution.py:402
  32.4 0.7 collective-permute-start.2
  33.1 1.3 %collective-permute-start.8 = (bf16[112,1024]{1,0:T(8,128)(2,1)S(1)}, bf16[112,1024]{1,0:T(8,128)(2,1)S(1)}, u32[]{:S(2)}, u32[]{:S(2)}) collective-permute-start(bf16[112,1024]{1,0:T(8,128)(2,1)S(1)} %get-tuple-element.73), channel_id=1, source_target_pairs={{16,24},{17,25},{18,26},{19,27},{20,28},{21,29},{22,30},{23,31}} | collective-permute-start | bytes 688136 | tf_op jit(solution)/shard_map/ppermute | solution.py:402
  34.4 0.7 collective-permute-start.7
  35.1 1.3 %collective-permute-start.14 = (bf16[112,1024]{1,0:T(8,128)(2,1)S(1)}, bf16[112,1024]{1,0:T(8,128)(2,1)S(1)}, u32[]{:S(2)}, u32[]{:S(2)}) collective-permute-start(bf16[112,1024]{1,0:T(8,128)(2,1)S(1)} %get-tuple-element.85), channel_id=1, source_target_pairs={{16,24},{17,25},{18,26},{19,27},{20,28},{21,29},{22,30},{23,31}} | collective-permute-start | bytes 688136 | tf_op jit(solution)/shard_map/ppermute | solution.py:402
  36.4 14.8 %collective-permute-done.10.incoming = bf16[112,1024]{1,0:T(8,128)(2,1)S(1)} collective-permute-done((bf16[112,1024]{1,0:T(8,128)(2,1)S(1)}, bf16[112,1024]{1,0:T(8,128)(2,1)S(1)}, u32[]{:S(2)}, u32[]{:S(2)}) %collective-permute-start.10) | collective-permute-done | bytes 229408 | tf_op jit(solution)/shard_map/ppermute | solution.py:402
  51.2 1.0 %last.5 = (f32[512,1024]{1,0:T(8,128)S(1)}, f32[512,1024]{1,0:T(8,128)}) custom-call(bf16[112,1024]{1,0:T(8,128)(2,1)S(1)} %collective-permute-done.10.incoming, f32[512,1024]{1,0:T(8,128)S(1)} %get-tuple-element.78.image, f32[512,1024]{1,0:T(8,128)S(1)} %get-tuple-element.58.turns), custom_call_target="tpu_custom_call", output_to_operand_aliasing={{0}: (1, {})} | custom-call | tf_op jit(solution)/shard_map/last/pallas_call | solution.py:457
  52.3 1.3 %collective-permute-start.13 = (bf16[112,1024]{1,0:T(8,128)(2,1)S(1)}, bf16[112,1024]{1,0:T(8,128)(2,1)S(1)}, u32[]{:S(2)}, u32[]{:S(2)}) collective-permute-start(bf16[112,1024]{1,0:T(8,128)(2,1)S(1)} %get-tuple-element.84), channel_id=1, source_target_pairs={{16,24},{17,25},{18,26},{19,27},{20,28},{21,29},{22,30},{23,31}} | collective-permute-start | bytes 688136 | tf_op jit(solution)/shard_map/ppermute | solution.py:402
  53.6 2.6 %collective-permute-done.8.incoming = bf16[112,1024]{1,0:T(8,128)(2,1)S(1)} collective-permute-done((bf16[112,1024]{1,0:T(8,128)(2,1)S(1)}, bf16[112,1024]{1,0:T(8,128)(2,1)S(1)}, u32[]{:S(2)}, u32[]{:S(2)}) %collective-permute-start.8) | collective-permute-done | bytes 229408 | tf_op jit(solution)/shard_map/ppermute | solution.py:402
  56.1 1.0 %last.6 = (f32[512,1024]{1,0:T(8,128)S(1)}, f32[512,1024]{1,0:T(8,128)}) custom-call(bf16[112,1024]{1,0:T(8,128)(2,1)S(1)} %collective-permute-done.8.incoming, f32[512,1024]{1,0:T(8,128)S(1)} %get-tuple-element.80.image, f32[512,1024]{1,0:T(8,128)S(1)} %get-tuple-element.58.turns, ...), custom_call_target="tpu_custom_call", output_to_operand_aliasing={{0}: (1, {}), {1}: (3, {})} | custom-call | tf_op jit(solution)/shard_map/last/pallas_call | solution.py:457
  57.2 1.3 %collective-permute-start.12 = (bf16[64,1024]{1,0:T(8,128)(2,1)S(1)}, bf16[64,1024]{1,0:T(8,128)(2,1)S(1)}, u32[]{:S(2)}, u32[]{:S(2)}) collective-permute-start(bf16[64,1024]{1,0:T(8,128)(2,1)S(1)} %get-tuple-element.83), channel_id=1, source_target_pairs={{16,24},{17,25},{18,26},{19,27},{20,28},{21,29},{22,30},{23,31}} | collective-permute-start | bytes 393224 | tf_op jit(solution)/shard_map/ppermute | solution.py:402
  58.5 2.6 %collective-permute-done.14.incoming = bf16[112,1024]{1,0:T(8,128)(2,1)S(1)} collective-permute-done((bf16[112,1024]{1,0:T(8,128)(2,1)S(1)}, bf16[112,1024]{1,0:T(8,128)(2,1)S(1)}, u32[]{:S(2)}, u32[]{:S(2)}) %collective-permute-start.14) | collective-permute-done | bytes 229408 | tf_op jit(solution)/shard_map/ppermute | solution.py:402
  61.0 1.0 %last.7 = (f32[512,1024]{1,0:T(8,128)S(1)}, f32[512,1024]{1,0:T(8,128)}) custom-call(bf16[112,1024]{1,0:T(8,128)(2,1)S(1)} %collective-permute-done.14.incoming, f32[512,1024]{1,0:T(8,128)S(1)} %get-tuple-element.86.image, f32[512,1024]{1,0:T(8,128)S(1)} %get-tuple-element.58.turns, ...), custom_call_target="tpu_custom_call", output_to_operand_aliasing={{0}: (1, {}), {1}: (3, {})} | custom-call | tf_op jit(solution)/shard_map/last/pallas_call | solution.py:457
  62.0 3.1 %collective-permute-done.13.incoming = bf16[112,1024]{1,0:T(8,128)(2,1)S(1)} collective-permute-done((bf16[112,1024]{1,0:T(8,128)(2,1)S(1)}, bf16[112,1024]{1,0:T(8,128)(2,1)S(1)}, u32[]{:S(2)}, u32[]{:S(2)}) %collective-permute-start.13) | collective-permute-done | bytes 229408 | tf_op jit(solution)/shard_map/ppermute | solution.py:402
  65.1 1.0 %last.8 = (f32[512,1024]{1,0:T(8,128)S(1)}, f32[512,1024]{1,0:T(8,128)}) custom-call(bf16[112,1024]{1,0:T(8,128)(2,1)S(1)} %collective-permute-done.13.incoming, f32[512,1024]{1,0:T(8,128)S(1)} %get-tuple-element.88.image, f32[512,1024]{1,0:T(8,128)S(1)} %get-tuple-element.58.turns, ...), custom_call_target="tpu_custom_call", output_to_operand_aliasing={{0}: (1, {}), {1}: (3, {})} | custom-call | tf_op jit(solution)/shard_map/last/pallas_call | solution.py:457
  66.1 0.4 collective-permute-done.12.incoming
  66.5 0.8 %last.9 = (f32[512,1024]{1,0:T(8,128)S(1)}, f32[512,1024]{1,0:T(8,128)}) custom-call(bf16[64,1024]{1,0:T(8,128)(2,1)S(1)} %collective-permute-done.12.incoming, f32[512,1024]{1,0:T(8,128)S(1)} %get-tuple-element.90.image, f32[512,1024]{1,0:T(8,128)S(1)} %get-tuple-element.58.turns, ...), custom_call_target="tpu_custom_call", output_to_operand_aliasing={{0}: (1, {}), {1}: (3, {})} | custom-call | tf_op jit(solution)/shard_map/last/pallas_call | solution.py:457
  (31 shorter events, 0.6 us)
Async XLA Ops:
  20.8 6.6 %collective-permute-start.1 = (bf16[112,1024]{1,0:T(8,128)(2,1)S(1)}, bf16[112,1024]{1,0:T(8,128)(2,1)S(1)}, u32[]{:S(2)}, u32[]{:S(2)}) collective-permute-start(bf16[112,1024]{1,0:T(8,128)(2,1)S(1)} %get-tuple-element.54), channel_id=1, source_target_pairs={{0,8},{1,9},{2,10},{3,11},{4,12},{5,13},{6,14},{7,15}} | collective-permute-start | bytes 688136 | tf_op jit(solution)/shard_map/ppermute | solution.py:402
  22.4 6.5 %collective-permute-start = (bf16[112,1024]{1,0:T(8,128)(2,1)S(1)}, bf16[112,1024]{1,0:T(8,128)(2,1)S(1)}, u32[]{:S(2)}, u32[]{:S(2)}) collective-permute-start(bf16[112,1024]{1,0:T(8,128)(2,1)S(1)} %get-tuple-element.53), channel_id=1, source_target_pairs={{0,8},{1,9},{2,10},{3,11},{4,12},{5,13},{6,14},{7,15}} | collective-permute-start | bytes 688136 | tf_op jit(solution)/shard_map/ppermute | solution.py:402
  23.1 1.5 %copy-start = (f32[1,512,512]{2,1,0:T(8,128)S(1)}, f32[1,512,512]{2,1,0:T(8,128)}, u32[]{:S(2)}) copy-start(f32[1,512,512]{2,1,0:T(8,128)} %param.11) | copy-start | bytes 3145732
  23.9 5.7 %collective-permute-start.6 = (bf16[112,1024]{1,0:T(8,128)(2,1)S(1)}, bf16[112,1024]{1,0:T(8,128)(2,1)S(1)}, u32[]{:S(2)}, u32[]{:S(2)}) collective-permute-start(bf16[112,1024]{1,0:T(8,128)(2,1)S(1)} %get-tuple-element.66), channel_id=1, source_target_pairs={{0,8},{1,9},{2,10},{3,11},{4,12},{5,13},{6,14},{7,15}} | collective-permute-start | bytes 688136 | tf_op jit(solution)/shard_map/ppermute | solution.py:402
  27.5 2.9 %collective-permute-start.5 = (bf16[112,1024]{1,0:T(8,128)(2,1)S(1)}, bf16[112,1024]{1,0:T(8,128)(2,1)S(1)}, u32[]{:S(2)}, u32[]{:S(2)}) collective-permute-start(bf16[112,1024]{1,0:T(8,128)(2,1)S(1)} %get-tuple-element.65), channel_id=1, source_target_pairs={{8,16},{9,17},{10,18},{11,19},{12,20},{13,21},{14,22},{15,23}} | collective-permute-start | bytes 688136 | tf_op jit(solution)/shard_map/ppermute | solution.py:402
  28.2 3.5 %collective-permute-start.4 = (bf16[112,1024]{1,0:T(8,128)(2,1)S(1)}, bf16[112,1024]{1,0:T(8,128)(2,1)S(1)}, u32[]{:S(2)}, u32[]{:S(2)}) collective-permute-start(bf16[112,1024]{1,0:T(8,128)(2,1)S(1)} %get-tuple-element.64), channel_id=1, source_target_pairs={{0,8},{1,9},{2,10},{3,11},{4,12},{5,13},{6,14},{7,15}} | collective-permute-start | bytes 688136 | tf_op jit(solution)/shard_map/ppermute | solution.py:402
  28.9 4.2 %collective-permute-start.3 = (bf16[112,1024]{1,0:T(8,128)(2,1)S(1)}, bf16[112,1024]{1,0:T(8,128)(2,1)S(1)}, u32[]{:S(2)}, u32[]{:S(2)}) collective-permute-start(bf16[112,1024]{1,0:T(8,128)(2,1)S(1)} %get-tuple-element.63), channel_id=1, source_target_pairs={{8,16},{9,17},{10,18},{11,19},{12,20},{13,21},{14,22},{15,23}} | collective-permute-start | bytes 688136 | tf_op jit(solution)/shard_map/ppermute | solution.py:402
  29.6 5.5 %collective-permute-start.11 = (bf16[112,1024]{1,0:T(8,128)(2,1)S(1)}, bf16[112,1024]{1,0:T(8,128)(2,1)S(1)}, u32[]{:S(2)}, u32[]{:S(2)}) collective-permute-start(bf16[112,1024]{1,0:T(8,128)(2,1)S(1)} %get-tuple-element.76), channel_id=1, source_target_pairs={{8,16},{9,17},{10,18},{11,19},{12,20},{13,21},{14,22},{15,23}} | collective-permute-start | bytes 688136 | tf_op jit(solution)/shard_map/ppermute | solution.py:402
  30.3 20.9 %collective-permute-start.10 = (bf16[112,1024]{1,0:T(8,128)(2,1)S(1)}, bf16[112,1024]{1,0:T(8,128)(2,1)S(1)}, u32[]{:S(2)}, u32[]{:S(2)}) collective-permute-start(bf16[112,1024]{1,0:T(8,128)(2,1)S(1)} %get-tuple-element.75), channel_id=1, source_target_pairs={{16,24},{17,25},{18,26},{19,27},{20,28},{21,29},{22,30},{23,31}} | collective-permute-start | bytes 688136 | tf_op jit(solution)/shard_map/ppermute | solution.py:402
  31.7 20.5 %collective-permute-start.9 = (bf16[112,1024]{1,0:T(8,128)(2,1)S(1)}, bf16[112,1024]{1,0:T(8,128)(2,1)S(1)}, u32[]{:S(2)}, u32[]{:S(2)}) collective-permute-start(bf16[112,1024]{1,0:T(8,128)(2,1)S(1)} %get-tuple-element.74), channel_id=1, source_target_pairs={{8,16},{9,17},{10,18},{11,19},{12,20},{13,21},{14,22},{15,23}} | collective-permute-start | bytes 688136 | tf_op jit(solution)/shard_map/ppermute | solution.py:402
  32.4 2.0 %collective-permute-start.2 = (bf16[64,1024]{1,0:T(8,128)(2,1)S(1)}, bf16[64,1024]{1,0:T(8,128)(2,1)S(1)}, u32[]{:S(2)}, u32[]{:S(2)}) collective-permute-start(bf16[64,1024]{1,0:T(8,128)(2,1)S(1)} %get-tuple-element.62), channel_id=1, source_target_pairs={{0,8},{1,9},{2,10},{3,11},{4,12},{5,13},{6,14},{7,15}} | collective-permute-start | bytes 393224 | tf_op jit(solution)/shard_map/ppermute | solution.py:402
  33.1 23.1 %collective-permute-start.8 = (bf16[112,1024]{1,0:T(8,128)(2,1)S(1)}, bf16[112,1024]{1,0:T(8,128)(2,1)S(1)}, u32[]{:S(2)}, u32[]{:S(2)}) collective-permute-start(bf16[112,1024]{1,0:T(8,128)(2,1)S(1)} %get-tuple-element.73), channel_id=1, source_target_pairs={{16,24},{17,25},{18,26},{19,27},{20,28},{21,29},{22,30},{23,31}} | collective-permute-start | bytes 688136 | tf_op jit(solution)/shard_map/ppermute | solution.py:402
  34.4 22.7 %collective-permute-start.7 = (bf16[64,1024]{1,0:T(8,128)(2,1)S(1)}, bf16[64,1024]{1,0:T(8,128)(2,1)S(1)}, u32[]{:S(2)}, u32[]{:S(2)}) collective-permute-start(bf16[64,1024]{1,0:T(8,128)(2,1)S(1)} %get-tuple-element.72), channel_id=1, source_target_pairs={{8,16},{9,17},{10,18},{11,19},{12,20},{13,21},{14,22},{15,23}} | collective-permute-start | bytes 393224 | tf_op jit(solution)/shard_map/ppermute | solution.py:402
  35.1 25.9 %collective-permute-start.14 = (bf16[112,1024]{1,0:T(8,128)(2,1)S(1)}, bf16[112,1024]{1,0:T(8,128)(2,1)S(1)}, u32[]{:S(2)}, u32[]{:S(2)}) collective-permute-start(bf16[112,1024]{1,0:T(8,128)(2,1)S(1)} %get-tuple-element.85), channel_id=1, source_target_pairs={{16,24},{17,25},{18,26},{19,27},{20,28},{21,29},{22,30},{23,31}} | collective-permute-start | bytes 688136 | tf_op jit(solution)/shard_map/ppermute | solution.py:402
  52.3 12.9 %collective-permute-start.13 = (bf16[112,1024]{1,0:T(8,128)(2,1)S(1)}, bf16[112,1024]{1,0:T(8,128)(2,1)S(1)}, u32[]{:S(2)}, u32[]{:S(2)}) collective-permute-start(bf16[112,1024]{1,0:T(8,128)(2,1)S(1)} %get-tuple-element.84), channel_id=1, source_target_pairs={{16,24},{17,25},{18,26},{19,27},{20,28},{21,29},{22,30},{23,31}} | collective-permute-start | bytes 688136 | tf_op jit(solution)/shard_map/ppermute | solution.py:402
  57.2 9.3 %collective-permute-start.12 = (bf16[64,1024]{1,0:T(8,128)(2,1)S(1)}, bf16[64,1024]{1,0:T(8,128)(2,1)S(1)}, u32[]{:S(2)}, u32[]{:S(2)}) collective-permute-start(bf16[64,1024]{1,0:T(8,128)(2,1)S(1)} %get-tuple-element.83), channel_id=1, source_target_pairs={{16,24},{17,25},{18,26},{19,27},{20,28},{21,29},{22,30},{23,31}} | collective-permute-start | bytes 393224 | tf_op jit(solution)/shard_map/ppermute | solution.py:402
